TPU v7x, 32 devices: a whole 2x2x4 slice. The times are simulated.
32 devices in a mesh: seq: 4 (over x, core), head: 2 (over y), dp: 4 (over z).
Axes of the slice: x: 2, y: 2, z: 4, core: 2. Of those that a mesh axis runs over, the one named last changes fastest.
Arguments:
- queries: bfloat16 [8192, 4096], P(('dp', 'seq'), 'head'), parts along dimension 0, may hold values from -6 to 6
- key_vectors: bfloat16 [8192, 4096], P(('dp', 'seq'), 'head'), parts along dimension 0, may hold values from -6 to 6
- value_vectors: bfloat16 [8192, 4096], P(('dp', 'seq'), 'head'), parts along dimension 0, may hold values from -13 to 13
- norm_gain: float32 [4096], P('head'), may hold values from 0.1 to 1.9
- cotangent: bfloat16 [8192, 4096], P(('dp', 'seq'), 'head'), parts along dimension 0, may hold values from -6 to 6
Outputs:
- layer_out: bfloat16 [8192, 4096], P(('dp', 'seq'), 'head'), parts along dimension 0
- grad_query: bfloat16 [8192, 4096], P(('dp', 'seq'), 'head'), parts along dimension 0
- grad_key: bfloat16 [8192, 4096], P(('dp', 'seq'), 'head'), parts along dimension 0
- grad_value: bfloat16 [8192, 4096], P(('dp', 'seq'), 'head'), parts along dimension 0
There are 4 independent parts, one for each index of `dp`. A program takes and returns all parts, laid end to end along the dimension named above; an argument that names none is the same for every part. Nothing has to cross between parts.
All inputs are finite; a program needn't handle non-finite values.
Results may differ from a plain program's by a relative error of at most 0.0058.
Values sent between devices are 32-bit elements; how exact they have to be, the bound alone decides.
A program may use at most 64 MiB of HBM per device.

v0:
```python
import jax
import jax.numpy as jnp
from jax import lax
from jax.sharding import PartitionSpec as P

HD = 128
FEAT = 4096


EPS = 1e-06


def from_behind(block, axis, distance):
    devices = range(lax.axis_size(axis))
    route = [(i - distance, i) for i in devices if i - distance in devices]
    return lax.ppermute(block, axis, route)


def forward_prefix(own_total):
    empty_state = jnp.zeros_like(own_total)

    def forward_relay_turn(turn_index, carried):
        moving, summed = carried
        moving = from_behind(moving, "seq", 1)
        return (moving, summed + moving)

    return lax.fori_loop(0, lax.axis_size("seq") - 1, forward_relay_turn, (own_total, empty_state))[
        1
    ]


def backward_suffix(own_total):
    empty_state = jnp.zeros_like(own_total)

    def backward_relay_turn(turn_index, carried):
        moving, summed = carried
        moving = from_behind(moving, "seq", -1)
        return (moving, summed + moving)

    return lax.fori_loop(
        0, lax.axis_size("seq") - 1, backward_relay_turn, (own_total, empty_state)
    )[1]


def per_device(queries, key_vectors, value_vectors, norm_gain, cotangent):
    tokens_here, features = queries.shape
    head_count = features // HD
    block_rows = min(512, tokens_here)
    block_count = tokens_here // block_rows
    block_shape = (block_count, block_rows, head_count, HD)
    query_blocks = queries.reshape(block_shape)
    key_blocks = key_vectors.reshape(block_shape)
    value_blocks = value_vectors.reshape(block_shape)
    positions = jnp.arange(block_rows)
    causal = positions[:, None] >= positions[None, :]
    local_kv = jnp.einsum(
        "nshd,nshe->nhde", key_blocks, value_blocks, preferred_element_type=jnp.float32
    )
    incoming = forward_prefix(jnp.sum(local_kv, axis=0))
    running = jnp.cumsum(local_kv, axis=0)
    prefix_state = incoming[None] + jnp.concatenate(
        [jnp.zeros_like(local_kv), running[:-1]], axis=0
    )
    prefix_low = prefix_state.astype(jnp.bfloat16)
    scores = jnp.einsum(
        "nthd,nshd->nhts", query_blocks, key_blocks, preferred_element_type=jnp.float32
    )
    block_weights = jnp.where(causal, scores, 0.0).astype(jnp.bfloat16)
    attended = jnp.einsum(
        "nthd,nhde->nthe", query_blocks, prefix_low, preferred_element_type=jnp.float32
    )
    attended = attended + jnp.einsum(
        "nhts,nshe->nthe", block_weights, value_blocks, preferred_element_type=jnp.float32
    )
    attended = attended.reshape(tokens_here, features)
    scaled_grad = cotangent.astype(jnp.float32) * norm_gain
    squares, inner = lax.psum(
        (jnp.sum(attended * attended, axis=1), jnp.sum(scaled_grad * attended, axis=1)), "head"
    )
    inverse_rms = lax.rsqrt(squares / FEAT + EPS)[:, None]
    inner = inner[:, None]
    layer_out = (attended * inverse_rms * norm_gain).astype(jnp.bfloat16)
    out_grad = (
        inverse_rms * (scaled_grad - attended * inner * inverse_rms * inverse_rms / FEAT)
    ).astype(jnp.bfloat16)
    grad_blocks = out_grad.reshape(block_shape)
    local_qg = jnp.einsum(
        "nthd,nthe->nhde", query_blocks, grad_blocks, preferred_element_type=jnp.float32
    )
    later_states = backward_suffix(jnp.sum(local_qg, axis=0))
    running_back = jnp.cumsum(local_qg[::-1], axis=0)[::-1]
    suffix_state = later_states[None] + jnp.concatenate(
        [running_back[1:], jnp.zeros_like(local_qg)], axis=0
    )
    suffix_low = suffix_state.astype(jnp.bfloat16)
    grad_scores = jnp.einsum(
        "nthe,nshe->nhts", grad_blocks, value_blocks, preferred_element_type=jnp.float32
    )
    grad_weights = jnp.where(causal, grad_scores, 0.0).astype(jnp.bfloat16)
    query_grad = jnp.einsum(
        "nthe,nhde->nthd", grad_blocks, prefix_low, preferred_element_type=jnp.float32
    )
    query_grad = query_grad + jnp.einsum(
        "nhts,nshd->nthd", grad_weights, key_blocks, preferred_element_type=jnp.float32
    )
    key_grad = jnp.einsum(
        "nshe,nhde->nshd", value_blocks, suffix_low, preferred_element_type=jnp.float32
    )
    key_grad = key_grad + jnp.einsum(
        "nhts,nthd->nshd", grad_weights, query_blocks, preferred_element_type=jnp.float32
    )
    value_grad = jnp.einsum(
        "nshd,nhde->nshe", key_blocks, suffix_low, preferred_element_type=jnp.float32
    )
    value_grad = value_grad + jnp.einsum(
        "nhts,nthe->nshe", block_weights, grad_blocks, preferred_element_type=jnp.float32
    )
    grad_query = query_grad.reshape(tokens_here, features).astype(jnp.bfloat16)
    grad_key = key_grad.reshape(tokens_here, features).astype(jnp.bfloat16)
    grad_value = value_grad.reshape(tokens_here, features).astype(jnp.bfloat16)
    return (layer_out, grad_query, grad_key, grad_value)


def solution(mesh):
    return jax.shard_map(
        per_device,
        mesh=mesh,
        in_specs=(
            P(("dp", "seq"), "head"),
            P(("dp", "seq"), "head"),
            P(("dp", "seq"), "head"),
            P("head"),
            P(("dp", "seq"), "head"),
        ),
        out_specs=(
            P(("dp", "seq"), "head"),
            P(("dp", "seq"), "head"),
            P(("dp", "seq"), "head"),
            P(("dp", "seq"), "head"),
        ),
        check_vma=False,
    )
```

profile of v0, /device:TPU:1, one launch (start us, length us, event | category | flops | bytes accessed | tf_op | source)
XLA Modules:
  0.0 217.8 jit_solution(17336007482986021173)
XLA Ops:
  0.6 4.1 %copy.36 = bf16[512,2048]{0,1:T(8,128)(2,1)} copy(bf16[512,2048]{1,0:T(8,128)(2,1)} %param.9) | data formatting | bytes 4194304 | tf_op jit(solution)/shard_map/reshape.5
  4.7 3.5 %copy.40 = bf16[64,8,16,128]{3,2,1,0:T(8,128)(2,1)} copy(bf16[64,8,16,128]{3,1,2,0:T(8,128)(2,1)} %bitcast.98) | data formatting | bytes 4194304
  8.3 4.3 %copy.9 = bf16[512,16,128]{0,2,1:T(8,128)(2,1)} copy(bf16[512,16,128]{2,1,0:T(8,128)(2,1)} %bitcast.99) | data formatting | bytes 4194304 | tf_op jit(solution)/shard_map/reshape
  12.5 3.3 %fusion.10 = f32[16,128,128]{2,1,0:T(8,128)} fusion(bf16[512,16,128]{0,2,1:T(8,128)(2,1)} %copy.9, bf16[512,2048]{1,0:T(8,128)(2,1)S(1)} %copy-done), kind=kOutput, calls=%fused_computation.23 | convolution fusion | flops 268435456 | bytes 5242880 | tf_op jit(solution)/shard_map/nshd,nshe->nhde/dot_general | solution.py:56
  15.8 56.1 %while.26 = (s32[]{:T(128)}, f32[16,128,128]{2,1,0:T(8,128)}, f32[16,128,128]{2,1,0:T(8,128)}, s32[]{:T(128)}, s32[]{:T(128)}) while((s32[]{:T(128)}, f32[16,128,128]{2,1,0:T(8,128)}, f32[16,128,128]{2,1,0:T(8,128)}, s32[]{:T(128)}, s32[]{:T(128)}) %tuple.47), condition=%wide.region_1.0_spmd.clone, body=%wide.region_0.0_spmd.clone.sunk | while | flops 524291 | bytes 17825960 | solution.py:27
  15.8 4.5 %collective-permute-start = (f32[16,128,128]{2,1,0:T(8,128)}, f32[16,128,128]{2,1,0:T(8,128)S(1)}, u32[]{:S(2)}, u32[]{:S(2)}) collective-permute-start(f32[16,128,128]{2,1,0:T(8,128)} %get-tuple-element.133), channel_id=1, source_target_pairs={{0,8},{8,16},{16,24},{1,9},{9,17},{17,25},{2,10},{10,18},{18,26},{... | collective-permute-start | bytes 3145736 | tf_op jit(solution)/shard_map/while/body/eval_jaxpr/ppermute | solution.py:16
  20.3 12.0 %collective-permute-done = f32[16,128,128]{2,1,0:T(8,128)S(1)} collective-permute-done((f32[16,128,128]{2,1,0:T(8,128)}, f32[16,128,128]{2,1,0:T(8,128)S(1)}, u32[]{:S(2)}, u32[]{:S(2)}) %collective-permute-start) | collective-permute-done | bytes 1048608 | tf_op jit(solution)/shard_map/while/body/eval_jaxpr/ppermute | solution.py:16
  34.7 4.3 %collective-permute-start = (f32[16,128,128]{2,1,0:T(8,128)}, f32[16,128,128]{2,1,0:T(8,128)S(1)}, u32[]{:S(2)}, u32[]{:S(2)}) collective-permute-start(f32[16,128,128]{2,1,0:T(8,128)} %get-tuple-element.133), channel_id=1, source_target_pairs={{0,8},{8,16},{16,24},{1,9},{9,17},{17,25},{2,10},{10,18},{18,26},{... | collective-permute-start | bytes 3145736 | tf_op jit(solution)/shard_map/while/body/eval_jaxpr/ppermute | solution.py:16
  39.0 12.0 %collective-permute-done = f32[16,128,128]{2,1,0:T(8,128)S(1)} collective-permute-done((f32[16,128,128]{2,1,0:T(8,128)}, f32[16,128,128]{2,1,0:T(8,128)S(1)}, u32[]{:S(2)}, u32[]{:S(2)}) %collective-permute-start) | collective-permute-done | bytes 1048608 | tf_op jit(solution)/shard_map/while/body/eval_jaxpr/ppermute | solution.py:16
  53.3 4.3 %collective-permute-start = (f32[16,128,128]{2,1,0:T(8,128)}, f32[16,128,128]{2,1,0:T(8,128)S(1)}, u32[]{:S(2)}, u32[]{:S(2)}) collective-permute-start(f32[16,128,128]{2,1,0:T(8,128)} %get-tuple-element.133), channel_id=1, source_target_pairs={{0,8},{8,16},{16,24},{1,9},{9,17},{17,25},{2,10},{10,18},{18,26},{... | collective-permute-start | bytes 3145736 | tf_op jit(solution)/shard_map/while/body/eval_jaxpr/ppermute | solution.py:16
  57.6 12.0 %collective-permute-done = f32[16,128,128]{2,1,0:T(8,128)S(1)} collective-permute-done((f32[16,128,128]{2,1,0:T(8,128)}, f32[16,128,128]{2,1,0:T(8,128)S(1)}, u32[]{:S(2)}, u32[]{:S(2)}) %collective-permute-start) | collective-permute-done | bytes 1048608 | tf_op jit(solution)/shard_map/while/body/eval_jaxpr/ppermute | solution.py:16
  71.9 2.8 %fusion.22 = f32[16,128,512]{2,1,0:T(8,128)S(1)} fusion(bf16[512,16,128]{0,2,1:T(8,128)(2,1)} %bitcast.89, f32[16,128,128]{2,1,0:T(8,128)} %get-tuple-element.38), kind=kOutput, calls=%fused_computation.37 | convolution fusion | flops 268697600 | bytes 7340032 | tf_op jit(solution)/shard_map/nthd,nhde->nthe/dot_general | solution.py:69
  75.1 5.9 %select_convert_fusion.1 = bf16[16,512,512]{2,1,0:T(8,128)(2,1)} fusion(bf16[512,16,128]{0,2,1:T(8,128)(2,1)S(1)} %bitcast.91, pred[512,512]{1,0:T(8,128)(4,1)S(1)} %iota_compare_fusion, bf16[512,2048]{1,0:T(8,128)(2,1)S(1)} %copy-done.13), kind=kOutput, calls=%fused_computation.3 | convolution fusion | flops 1082130432 | bytes 12845056 | tf_op jit(solution)/shard_map/nthd,nshd->nhts/dot_general | solution.py:65
  80.9 8.2 %fusion.2 = (f32[512]{0:T(512)S(1)}, f32[16,128,512]{2,1,0:T(8,128)}) fusion(f32[16,128,512]{2,1,0:T(8,128)S(1)} %fusion.22, bf16[16,512,512]{2,1,0:T(8,128)(2,1)} %select_convert_fusion.1, bf16[512,2048]{1,0:T(8,128)(2,1)S(1)} %copy-done), kind=kOutput, calls=%fused_computation.9 | convolution fusion | flops 1076887040 | bytes 18876416 | tf_op jit(solution)/shard_map/nhts,nshe->nthe/dot_general | solution.py:72
  89.2 5.4 %copy.16 = f32[512,2048]{1,0:T(8,128)} copy(f32[512,2048]{0,1:T(8,128)} %bitcast.97) | data formatting | bytes 8388608 | tf_op jit(solution)/shard_map/reshape | solution.py:75
  94.6 3.5 %multiply_reduce_fusion = f32[512]{0:T(512)S(1)} fusion(f32[512,2048]{1,0:T(8,128)} %copy.16, bf16[512,2048]{1,0:T(8,128)(2,1)} %param.13, f32[2048]{0:T(1024)S(1)} %copy-done.14), kind=kLoop, calls=%fused_computation.13 | loop fusion | flops 4193792 | bytes 6301696 | tf_op jit(solution)/shard_map/reduce_sum | solution.py:78
  98.1 4.0 %all-reduce = (f32[512]{0:T(512)S(1)}, f32[512]{0:T(512)S(1)}) all-reduce(f32[512]{0:T(512)S(1)} %get-tuple-element.87, f32[512]{0:T(512)S(1)} %multiply_reduce_fusion), channel_id=1, replica_groups=mesh['seq'=4,'head'=2,'dp'=4] {'head'}, use_global_device_ids=true, to_apply=%region_3.0 | all-reduce | flops 1024 | bytes 8192 | tf_op jit(solution)/shard_map/psum | solution.py:77
  102.1 5.6 %multiply_convert_fusion = (bf16[512,2048]{1,0:T(8,128)(2,1)}, bf16[512,2048]{1,0:T(8,128)(2,1)}) fusion(f32[512,2048]{1,0:T(8,128)} %copy.16, bf16[512,2048]{1,0:T(8,128)(2,1)} %param.13, f32[512]{0:T(512)S(1)} %get-tuple-element.84, f32[2048]{0:T(1024)S(1)} %copy-done.14, f32[512]{0:T(512)S(1)} %add_rsqrt_fusion), kind=kLoop, calls=%fused_computation.12 | loop fusion | flops 12582912 | bytes 10498048 | tf_op jit(solution)/shard_map/convert_element_type | solution.py:85
  107.7 3.9 %copy.37 = bf16[512,2048]{0,1:T(8,128)(2,1)} copy(bf16[512,2048]{1,0:T(8,128)(2,1)} %get-tuple-element.85) | data formatting | bytes 4194304 | tf_op jit(solution)/shard_map/reshape.26
  111.6 2.9 %convolution_bitcast_fusion = f32[16,128,128]{1,2,0:T(8,128)S(1)} fusion(bf16[512,16,128]{0,2,1:T(8,128)(2,1)} %bitcast.93, bf16[512,16,128]{0,2,1:T(8,128)(2,1)} %bitcast.90), kind=kOutput, calls=%fused_computation.27 | convolution fusion | flops 268435456 | bytes 5242880 | tf_op jit(solution)/shard_map/nthd,nthe->nhde/dot_general | solution.py:87
  115.8 57.7 %while.27 = (s32[]{:T(128)}, f32[16,128,128]{2,1,0:T(8,128)}, f32[16,128,128]{2,1,0:T(8,128)}, s32[]{:T(128)}, s32[]{:T(128)}) while((s32[]{:T(128)}, f32[16,128,128]{2,1,0:T(8,128)}, f32[16,128,128]{2,1,0:T(8,128)}, s32[]{:T(128)}, s32[]{:T(128)}) %tuple.50), condition=%wide.region_7.8_spmd.clone, body=%wide.region_6.7_spmd.clone.sunk | while | flops 524291 | bytes 17825960 | solution.py:40
  117.8 16.2 %collective-permute-done.1 = f32[16,128,128]{2,1,0:T(8,128)S(1)} collective-permute-done((f32[16,128,128]{2,1,0:T(8,128)}, f32[16,128,128]{2,1,0:T(8,128)S(1)}, u32[]{:S(2)}, u32[]{:S(2)}) %collective-permute-start.1) | collective-permute-done | bytes 1048608 | tf_op jit(solution)/shard_map/while/body/eval_jaxpr/ppermute | solution.py:16
  138.2 14.4 %collective-permute-done.1 = f32[16,128,128]{2,1,0:T(8,128)S(1)} collective-permute-done((f32[16,128,128]{2,1,0:T(8,128)}, f32[16,128,128]{2,1,0:T(8,128)S(1)}, u32[]{:S(2)}, u32[]{:S(2)}) %collective-permute-start.1) | collective-permute-done | bytes 1048608 | tf_op jit(solution)/shard_map/while/body/eval_jaxpr/ppermute | solution.py:16
  156.8 14.4 %collective-permute-done.1 = f32[16,128,128]{2,1,0:T(8,128)S(1)} collective-permute-done((f32[16,128,128]{2,1,0:T(8,128)}, f32[16,128,128]{2,1,0:T(8,128)S(1)}, u32[]{:S(2)}, u32[]{:S(2)}) %collective-permute-start.1) | collective-permute-done | bytes 1048608 | tf_op jit(solution)/shard_map/while/body/eval_jaxpr/ppermute | solution.py:16
  173.5 2.8 %fusion.3 = f32[16,128,512]{2,1,0:T(8,128)S(1)} fusion(f32[16,128,128]{2,1,0:T(8,128)} %get-tuple-element.39, bf16[512,2048]{1,0:T(8,128)(2,1)} %param.10), kind=kOutput, calls=%fused_computation.16 | convolution fusion | flops 268697600 | bytes 7340032 | tf_op jit(solution)/shard_map/nshd,nhde->nshe/dot_general | solution.py:112
  176.4 6.2 %add_convert_fusion = bf16[16,128,512]{2,1,0:T(8,128)(2,1)} fusion(f32[16,128,512]{2,1,0:T(8,128)S(1)} %fusion.3, bf16[512,16,128]{0,2,1:T(8,128)(2,1)S(1)} %bitcast.95, bf16[16,512,512]{2,1,0:T(8,128)(2,1)} %select_convert_fusion.1), kind=kOutput, calls=%fused_computation.11 | convolution fusion | flops 1075838976 | bytes 16777216 | tf_op jit(solution)/shard_map/nhts,nthe->nshe/dot_general | solution.py:115
  182.6 4.0 %copy.33 = bf16[512,2048]{1,0:T(8,128)(2,1)} copy(bf16[512,2048]{0,1:T(8,128)(2,1)} %bitcast.101) | data formatting | bytes 4194304
  186.6 2.7 %fusion.7 = f32[16,128,512]{2,1,0:T(8,128)} fusion(f32[16,128,128]{2,1,0:T(8,128)S(1)} %copy-done.6, bf16[512,2048]{1,0:T(8,128)(2,1)S(1)} %copy-done), kind=kOutput, calls=%fused_computation.20 | convolution fusion | flops 268697600 | bytes 7340032 | tf_op jit(solution)/shard_map/nshe,nhde->nshd/dot_general | solution.py:106
  191.9 8.0 %fusion = bf16[16,128,512]{2,1,0:T(8,128)(2,1)} fusion(f32[16,128,512]{2,1,0:T(8,128)} %fusion.7, bf16[512,16,128]{0,2,1:T(8,128)(2,1)S(1)} %bitcast.92, bf16[16,512,512]{2,1,0:T(8,128)(2,1)S(1)} %select_convert_fusion), kind=kOutput, calls=%fused_computation.5 | convolution fusion | flops 1075838976 | bytes 16777216 | tf_op jit(solution)/shard_map/nhts,nthd->nshd/dot_general | solution.py:109
  199.9 4.0 %copy.32 = bf16[512,2048]{1,0:T(8,128)(2,1)} copy(bf16[512,2048]{0,1:T(8,128)(2,1)} %bitcast.102) | data formatting | bytes 4194304
  206.3 7.6 %fusion.1 = bf16[16,128,512]{2,1,0:T(8,128)(2,1)} fusion(f32[16,128,512]{2,1,0:T(8,128)S(1)} %fusion.20, bf16[16,512,512]{2,1,0:T(8,128)(2,1)} %copy-done.7, bf16[512,16,128]{0,2,1:T(8,128)(2,1)S(1)} %copy-done.12), kind=kOutput, calls=%fused_computation.7 | convolution fusion | flops 1075838976 | bytes 16777216 | tf_op jit(solution)/shard_map/nhts,nshd->nthd/dot_general | solution.py:103
  213.9 3.9 %copy.31 = bf16[512,2048]{1,0:T(8,128)(2,1)} copy(bf16[512,2048]{0,1:T(8,128)(2,1)} %bitcast.100) | data formatting | bytes 4194304
  (68 shorter events, 26.2 us)
Async XLA Ops:
  0.6 11.9 %copy-start = (bf16[512,2048]{1,0:T(8,128)(2,1)S(1)}, bf16[512,2048]{1,0:T(8,128)(2,1)}, u32[]{:S(2)}) copy-start(bf16[512,2048]{1,0:T(8,128)(2,1)} %param.11) | copy-start | bytes 6291460
  15.8 16.5 %collective-permute-start = (f32[16,128,128]{2,1,0:T(8,128)}, f32[16,128,128]{2,1,0:T(8,128)S(1)}, u32[]{:S(2)}, u32[]{:S(2)}) collective-permute-start(f32[16,128,128]{2,1,0:T(8,128)} %get-tuple-element.133), channel_id=1, source_target_pairs={{0,8},{8,16},{16,24},{1,9},{9,17},{17,25},{2,10},{10,18},{18,26},{... | collective-permute-start | bytes 3145736 | tf_op jit(solution)/shard_map/while/body/eval_jaxpr/ppermute | solution.py:16
  20.3 13.0 %copy-start.1 = (f32[16,128,128]{2,1,0:T(8,128)S(1)}, f32[16,128,128]{2,1,0:T(8,128)}, u32[]{:S(2)}) copy-start(f32[16,128,128]{2,1,0:T(8,128)} %get-tuple-element.134) | copy-start | bytes 3145732 | tf_op jit(solution)/shard_map/while
  33.7 1.0 copy-start.2
  34.7 16.3 %collective-permute-start = (f32[16,128,128]{2,1,0:T(8,128)}, f32[16,128,128]{2,1,0:T(8,128)S(1)}, u32[]{:S(2)}, u32[]{:S(2)}) collective-permute-start(f32[16,128,128]{2,1,0:T(8,128)} %get-tuple-element.133), channel_id=1, source_target_pairs={{0,8},{8,16},{16,24},{1,9},{9,17},{17,25},{2,10},{10,18},{18,26},{... | collective-permute-start | bytes 3145736 | tf_op jit(solution)/shard_map/while/body/eval_jaxpr/ppermute | solution.py:16
  38.9 13.0 %copy-start.1 = (f32[16,128,128]{2,1,0:T(8,128)S(1)}, f32[16,128,128]{2,1,0:T(8,128)}, u32[]{:S(2)}) copy-start(f32[16,128,128]{2,1,0:T(8,128)} %get-tuple-element.134) | copy-start | bytes 3145732 | tf_op jit(solution)/shard_map/while
  52.3 1.0 copy-start.2
  53.3 16.3 %collective-permute-start = (f32[16,128,128]{2,1,0:T(8,128)}, f32[16,128,128]{2,1,0:T(8,128)S(1)}, u32[]{:S(2)}, u32[]{:S(2)}) collective-permute-start(f32[16,128,128]{2,1,0:T(8,128)} %get-tuple-element.133), channel_id=1, source_target_pairs={{0,8},{8,16},{16,24},{1,9},{9,17},{17,25},{2,10},{10,18},{18,26},{... | collective-permute-start | bytes 3145736 | tf_op jit(solution)/shard_map/while/body/eval_jaxpr/ppermute | solution.py:16
  57.6 13.0 %copy-start.1 = (f32[16,128,128]{2,1,0:T(8,128)S(1)}, f32[16,128,128]{2,1,0:T(8,128)}, u32[]{:S(2)}) copy-start(f32[16,128,128]{2,1,0:T(8,128)} %get-tuple-element.134) | copy-start | bytes 3145732 | tf_op jit(solution)/shard_map/while
  70.9 1.0 copy-start.2
  71.9 2.9 %copy-start.8 = (bf16[512,2048]{0,1:T(8,128)(2,1)S(1)}, bf16[512,2048]{0,1:T(8,128)(2,1)}, u32[]{:S(2)}) copy-start(bf16[512,2048]{0,1:T(8,128)(2,1)} %copy.36) | copy-start | bytes 6291460
  71.9 3.2 %copy-start.13 = (bf16[512,2048]{1,0:T(8,128)(2,1)S(1)}, bf16[512,2048]{1,0:T(8,128)(2,1)}, u32[]{:S(2)}) copy-start(bf16[512,2048]{1,0:T(8,128)(2,1)} %param.10) | copy-start | bytes 6291460
  89.2 5.4 %copy-start.14 = (f32[2048]{0:T(1024)S(1)}, f32[2048]{0:T(1024)}, u32[]{:S(2)}) copy-start(f32[2048]{0:T(1024)} %param.12) | copy-start | bytes 24580
  115.8 18.1 %collective-permute-start.1 = (f32[16,128,128]{2,1,0:T(8,128)}, f32[16,128,128]{2,1,0:T(8,128)S(1)}, u32[]{:S(2)}, u32[]{:S(2)}) collective-permute-start(f32[16,128,128]{2,1,0:T(8,128)} %get-tuple-element.148), channel_id=1, source_target_pairs={{8,0},{16,8},{24,16},{9,1},{17,9},{25,17},{10,2},{18,10},{26,18},{... | collective-permute-start | bytes 3145736 | tf_op jit(solution)/shard_map/while/body/eval_jaxpr/ppermute | solution.py:16
  117.8 17.2 %copy-start.4 = (f32[16,128,128]{2,1,0:T(8,128)S(1)}, f32[16,128,128]{2,1,0:T(8,128)}, u32[]{:S(2)}) copy-start(f32[16,128,128]{2,1,0:T(8,128)} %get-tuple-element.149) | copy-start | bytes 3145732 | tf_op jit(solution)/shard_map/while
  135.3 1.0 copy-start.5
  136.3 16.3 %collective-permute-start.1 = (f32[16,128,128]{2,1,0:T(8,128)}, f32[16,128,128]{2,1,0:T(8,128)S(1)}, u32[]{:S(2)}, u32[]{:S(2)}) collective-permute-start(f32[16,128,128]{2,1,0:T(8,128)} %get-tuple-element.148), channel_id=1, source_target_pairs={{8,0},{16,8},{24,16},{9,1},{17,9},{25,17},{10,2},{18,10},{26,18},{... | collective-permute-start | bytes 3145736 | tf_op jit(solution)/shard_map/while/body/eval_jaxpr/ppermute | solution.py:16
  138.2 15.4 %copy-start.4 = (f32[16,128,128]{2,1,0:T(8,128)S(1)}, f32[16,128,128]{2,1,0:T(8,128)}, u32[]{:S(2)}) copy-start(f32[16,128,128]{2,1,0:T(8,128)} %get-tuple-element.149) | copy-start | bytes 3145732 | tf_op jit(solution)/shard_map/while
  153.9 1.0 copy-start.5
  154.9 16.3 %collective-permute-start.1 = (f32[16,128,128]{2,1,0:T(8,128)}, f32[16,128,128]{2,1,0:T(8,128)S(1)}, u32[]{:S(2)}, u32[]{:S(2)}) collective-permute-start(f32[16,128,128]{2,1,0:T(8,128)} %get-tuple-element.148), channel_id=1, source_target_pairs={{8,0},{16,8},{24,16},{9,1},{17,9},{25,17},{10,2},{18,10},{26,18},{... | collective-permute-start | bytes 3145736 | tf_op jit(solution)/shard_map/while/body/eval_jaxpr/ppermute | solution.py:16
  156.8 15.4 %copy-start.4 = (f32[16,128,128]{2,1,0:T(8,128)S(1)}, f32[16,128,128]{2,1,0:T(8,128)}, u32[]{:S(2)}) copy-start(f32[16,128,128]{2,1,0:T(8,128)} %get-tuple-element.149) | copy-start | bytes 3145732 | tf_op jit(solution)/shard_map/while
  172.5 1.0 copy-start.5
  173.5 2.8 %copy-start.10 = (bf16[512,2048]{0,1:T(8,128)(2,1)S(1)}, bf16[512,2048]{0,1:T(8,128)(2,1)}, u32[]{:S(2)}) copy-start(bf16[512,2048]{0,1:T(8,128)(2,1)} %copy.37) | copy-start | bytes 6291460
  182.6 4.0 %copy-start.6 = (f32[16,128,128]{2,1,0:T(8,128)S(1)}, f32[16,128,128]{2,1,0:T(8,128)}, u32[]{:S(2)}) copy-start(f32[16,128,128]{2,1,0:T(8,128)} %get-tuple-element.39) | copy-start | bytes 3145732
  186.6 2.7 %copy-start.11 = (bf16[512,2048]{0,1:T(8,128)(2,1)S(1)}, bf16[512,2048]{0,1:T(8,128)(2,1)}, u32[]{:S(2)}) copy-start(bf16[512,2048]{0,1:T(8,128)(2,1)} %copy.37) | copy-start | bytes 6291460
  189.3 2.6 %copy-start.9 = (bf16[512,2048]{0,1:T(8,128)(2,1)S(1)}, bf16[512,2048]{0,1:T(8,128)(2,1)}, u32[]{:S(2)}) copy-start(bf16[512,2048]{0,1:T(8,128)(2,1)} %copy.36) | copy-start | bytes 6291460
  191.9 8.0 %copy-start.7 = (bf16[16,512,512]{2,1,0:T(8,128)(2,1)}, bf16[16,512,512]{2,1,0:T(8,128)(2,1)S(1)}, u32[]{:S(2)}) copy-start(bf16[16,512,512]{2,1,0:T(8,128)(2,1)S(1)} %select_convert_fusion) | copy-start | bytes 25165828
  199.9 4.0 %copy-start.3 = (f32[16,128,128]{2,1,0:T(8,128)S(1)}, f32[16,128,128]{2,1,0:T(8,128)}, u32[]{:S(2)}) copy-start(f32[16,128,128]{2,1,0:T(8,128)} %get-tuple-element.38) | copy-start | bytes 3145732
  203.9 2.4 %copy-start.12 = (bf16[512,16,128]{0,2,1:T(8,128)(2,1)S(1)}, bf16[512,16,128]{0,2,1:T(8,128)(2,1)}, u32[]{:S(2)}) copy-start(bf16[512,16,128]{0,2,1:T(8,128)(2,1)} %copy.9) | copy-start | bytes 6291460
where the time goes:
time: 219 us; the launch traced here: 218 us
  waiting for transfers between devices  81 us (37%)
  matrix products  55.4 us (25%)
  local copies, waits for them, and re-layouts  46.4 us (21%)
  starting transfers between devices  18.8 us (9%)
  other arithmetic  11.3 us (5%)
  blocking collectives  3.97 us (2%)
    ppermute x6, waiting for transfers between devices, from_behind(): return lax.ppermute(block, axis, route)  81 us
    ppermute x6, starting transfers between devices, from_behind(): return lax.ppermute(block, axis, route)  18.8 us
    unnamed x27, local copies, waits for them, and re-layouts  17.1 us
    while x30, local copies, waits for them, and re-layouts  11.7 us
    dot_general x1, matrix products, per_device(): jnp.einsum('nhts,nshe->nthe', block_weights, value_blocks, preferred_elem...  8.24 us
    another operation x2, local copies, waits for them, and re-layouts  7.98 us
    dot_general x1, matrix products, per_device(): jnp.einsum('nhts,nthd->nshd', grad_weights, query_blocks, preferred_eleme...  7.96 us
    dot_general x1, matrix products, per_device(): jnp.einsum('nhts,nshd->nthd', grad_weights, key_blocks, preferred_element...  7.57 us
  transfers between devices with their start and end apart: 6, of which 6 were waited for; matrix products, arithmetic and copies ran while one was open for 0% of the time, Pallas kernels for 0%

commit v1 on v0

v1 whole, which is shorter than its diff:
```python
import functools

import jax
import jax.numpy as jnp
from jax import lax
from jax.experimental import pallas as pl
from jax.experimental.pallas import tpu as pltpu
from jax.sharding import PartitionSpec as P

HD = 128
PAIR = 2 * HD
FEAT = 4096
EPS = 1e-06
MESH = pl.DeviceIdType.MESH
F32 = jnp.float32
BF16 = jnp.bfloat16


def dot(a, b, a_dim, b_dim):
    return lax.dot_general(a, b, (((a_dim,), (b_dim,)), ((), ())), preferred_element_type=F32)


def block_diagonal(first, second):
    empty = jnp.zeros_like(first)
    return jnp.concatenate(
        [jnp.concatenate([first, empty], axis=1), jnp.concatenate([empty, second], axis=1)], axis=0
    )


def kernel(
    seq_size, head_size,
    q_hbm, k_hbm, v_hbm, gain_ref, ct_hbm,
    lo_hbm, gq_hbm, gk_hbm, gv_hbm,
    q, k, v, ct, lo, gq, gk, gv,
    weights, att, og, part_k, part_v,
    local, inner_in, total, cross_in, outer, prefix, acc_sq, acc_in, stat_out, stat_in,
    kv_sem, in_sem, out_sem, grad_sem,
    in_send, in_recv, cross_send, cross_recv, fwd_send, fwd_recv, stat_send, stat_recv,
):
    tokens, columns = q.shape
    tile = tokens // 2
    units = columns // PAIR
    half = units // 2
    chips = seq_size // 2
    me = lax.axis_index("seq")
    chip, core = me // 2, me % 2
    head = lax.axis_index("head")
    partner = chip * 2 + 1 - core

    def cols(unit):
        return pl.ds(pl.multiple_of(unit * PAIR, PAIR), PAIR)

    def own_unit(j):
        return core * half + j

    def other_unit(j):
        return (1 - core) * half + j

    def load(i, which):
        unit = lax.rem((1 - core) * half + i, units)
        source, target = ((k_hbm, k), (v_hbm, v))[which]
        return pltpu.make_async_copy(
            source.at[:, cols(unit)], target.at[:, cols(unit)], kv_sem.at[which, i]
        )

    def start_load(i, carry):
        load(i, 0).start()
        load(i, 1).start()
        return carry

    lax.fori_loop(0, units, start_load, 0)
    load_q = pltpu.make_async_copy(q_hbm, q, in_sem.at[0])
    load_ct = pltpu.make_async_copy(ct_hbm, ct, in_sem.at[1])
    load_q.start()
    load_ct.start()

    barrier = pltpu.get_barrier_semaphore()
    pl.semaphore_signal(barrier, inc=1, device_id={"seq": partner}, device_id_type=MESH)
    for d in range(1, chips):
        pl.semaphore_signal(
            barrier, inc=1, device_id={"seq": lax.rem(me + 2 * d, seq_size)}, device_id_type=MESH
        )
    for d in range(1, head_size):
        pl.semaphore_signal(
            barrier, inc=1, device_id={"head": lax.rem(head + d, head_size)}, device_id_type=MESH
        )
    pl.semaphore_wait(barrier, 1 + (chips - 1) + (head_size - 1))

    def states(unit):
        return pl.ds(2 * unit, 2)

    def to_partner(way, i):
        unit = lax.rem((1 - core) * half + i, units)
        return pltpu.make_async_remote_copy(
            src_ref=local.at[way, states(unit)],
            dst_ref=inner_in.at[way, states(unit)],
            send_sem=in_send.at[way, i],
            recv_sem=in_recv.at[way, i],
            device_id={"seq": partner},
            device_id_type=MESH,
        )

    def across(way, d, j):
        step = 2 * d if way == 0 else -2 * d
        return pltpu.make_async_remote_copy(
            src_ref=total.at[way, states(j)],
            dst_ref=cross_in.at[way, d - 1, states(j)],
            send_sem=cross_send.at[way, d - 1, j],
            recv_sem=cross_recv.at[way, d - 1, j],
            device_id={"seq": lax.rem(me + step + seq_size, seq_size)},
            device_id_type=MESH,
        )

    def forward(way, j, unit):
        return pltpu.make_async_remote_copy(
            src_ref=outer.at[way, states(unit)],
            dst_ref=outer.at[way, states(unit)],
            send_sem=fwd_send.at[way, j],
            recv_sem=fwd_recv.at[way, j],
            device_id={"seq": partner},
            device_id_type=MESH,
        )

    def sends_to(way, d):
        return chip + d < chips if way == 0 else chip - d >= 0

    def takes_from(way, d):
        return chip - d >= 0 if way == 0 else chip + d < chips

    def takes_any(way):
        return chip > 0 if way == 0 else chip < chips - 1

    def gives_inner(way):
        return core == 0 if way == 0 else core == 1

    def send_states(way, make):
        def partner_half(i, carry):
            make(i, other_unit(i))
            to_partner(way, i).start()
            return carry

        lax.fori_loop(0, half, partner_half, 0)

        def own_half(j, carry):
            unit = own_unit(j)
            make(half + j, unit)

            @pl.when(gives_inner(way))
            def _():
                to_partner(way, half + j).start()

            to_partner(way, j).wait_recv()
            total[way, states(j)] = local[way, states(unit)] + inner_in[way, states(unit)]
            for d in range(1, chips):

                @pl.when(sends_to(way, d))
                def _():
                    across(way, d, j).start()

            return carry

        lax.fori_loop(0, half, own_half, 0)

    def take_states(way, use):
        def step(j, carry):
            unit = own_unit(j)

            @pl.when(takes_any(way))
            def _():
                outer[way, states(unit)] = jnp.zeros((2, HD, HD), F32)
                for d in range(1, chips):

                    @pl.when(takes_from(way, d))
                    def _():
                        across(way, d, j).wait_recv()
                        outer[way, states(unit)] += cross_in[way, d - 1, states(j)]

                forward(way, j, unit).start()

            @pl.when(jnp.logical_not(takes_any(way)))
            def _():
                outer[way, states(unit)] = jnp.zeros((2, HD, HD), F32)
                outer[way, states(other_unit(j))] = jnp.zeros((2, HD, HD), F32)

            use(unit, low_state(way, unit))

            @pl.when(takes_any(way))
            def _():
                forward(way, j, other_unit(j)).wait_recv()

            @pl.when(jnp.logical_not(gives_inner(way)))
            def _():
                to_partner(way, half + j).wait_recv()

            use(other_unit(j), low_state(way, other_unit(j)))
            return carry

        lax.fori_loop(0, half, step, 0)

    def low_state(way, unit):
        state = outer[way, states(unit)]
        state = jnp.where(gives_inner(way), state, state + inner_in[way, states(unit)])
        state = state.astype(BF16)
        return block_diagonal(state[0], state[1])

    def end_sends(way):
        def step(j, carry):
            to_partner(way, j).wait_send()

            @pl.when(gives_inner(way))
            def _():
                to_partner(way, half + j).wait_send()

            for d in range(1, chips):

                @pl.when(sends_to(way, d))
                def _():
                    across(way, d, j).wait_send()

            @pl.when(takes_any(way))
            def _():
                forward(way, j, own_unit(j)).wait_send()

            return carry

        lax.fori_loop(0, half, step, 0)

    def make_kv(i, unit):
        load(i, 0).wait()
        load(i, 1).wait()
        key, value = k[:, cols(unit)], v[:, cols(unit)]
        for n in range(2):
            at = slice(n * HD, (n + 1) * HD)
            local[0, 2 * unit + n] = dot(key[:, at], value[:, at], 0, 0)

    send_states(0, make_kv)

    causal = lax.broadcasted_iota(jnp.int32, (tile, tile), 0) >= lax.broadcasted_iota(
        jnp.int32, (tile, tile), 1
    )

    def masked(scores):
        return jnp.where(causal, scores, 0.0).astype(BF16)

    acc_sq[...] = jnp.zeros_like(acc_sq)
    acc_in[...] = jnp.zeros_like(acc_in)
    load_q.wait()

    def own_scores(unit, carry):
        query, key, value = q[:, cols(unit)], k[:, cols(unit)], v[:, cols(unit)]
        for n in range(2):
            at = slice(n * HD, (n + 1) * HD)
            qh, kh, vh = query[:, at], key[:, at], value[:, at]
            w00 = masked(dot(qh[:tile], kh[:tile], 1, 1))
            w10 = dot(qh[tile:], kh[:tile], 1, 1).astype(BF16)
            w11 = masked(dot(qh[tile:], kh[tile:], 1, 1))
            weights[2 * unit + n, 0] = w00
            weights[2 * unit + n, 1] = w10
            weights[2 * unit + n, 2] = w11
            where = pl.ds(pl.multiple_of(unit * PAIR + n * HD, HD), HD)
            att[:tile, where] = dot(w00, vh[:tile], 1, 0)
            att[tile:, where] = dot(jnp.concatenate([w10, w11], axis=1), vh, 1, 0)
        return carry

    lax.fori_loop(0, units, own_scores, 0)
    load_ct.wait()

    def add_prefix(unit, low):
        prefix[unit] = low
        attended = att[:, cols(unit)] + dot(q[:, cols(unit)], low, 1, 0)
        att[:, cols(unit)] = attended
        squared = attended * attended
        product = ct[:, cols(unit)].astype(F32) * gain_ref[:, cols(unit)] * attended
        acc_sq[...] += squared[:, :HD] + squared[:, HD:]
        acc_in[...] += product[:, :HD] + product[:, HD:]

    take_states(0, add_prefix)

    stat_out[0:1, :] = jnp.sum(acc_sq[...].T, axis=0, keepdims=True)
    stat_out[1:2, :] = jnp.sum(acc_in[...].T, axis=0, keepdims=True)
    stat_out[2:8, :] = jnp.zeros((6, tokens), F32)

    def stat_copy(d):
        return pltpu.make_async_remote_copy(
            src_ref=stat_out,
            dst_ref=stat_in.at[d - 1],
            send_sem=stat_send.at[d - 1],
            recv_sem=stat_recv.at[d - 1],
            device_id={"head": lax.rem(head + d, head_size)},
            device_id_type=MESH,
        )

    for d in range(1, head_size):
        stat_copy(d).start()
    sums = stat_out[...]
    for d in range(1, head_size):
        stat_copy(d).wait_recv()
        sums = sums + stat_in[d - 1]
    inverse = lax.rsqrt(sums[0:1] / FEAT + EPS)
    scale = sums[1:2] * inverse * inverse * inverse / FEAT
    acc_sq[...] = jnp.broadcast_to(inverse, (HD, tokens)).T
    acc_in[...] = jnp.broadcast_to(scale, (HD, tokens)).T

    def make_qg(i, unit):
        gain = gain_ref[:, cols(unit)]
        inv = jnp.concatenate([acc_sq[...]] * 2, axis=1)
        coef = jnp.concatenate([acc_in[...]] * 2, axis=1)
        attended = att[:, cols(unit)]
        scaled = ct[:, cols(unit)].astype(F32) * gain
        out_grad = (inv * scaled - attended * coef).astype(BF16)
        og[:, cols(unit)] = out_grad
        query = q[:, cols(unit)]
        for n in range(2):
            at = slice(n * HD, (n + 1) * HD)
            local[1, 2 * unit + n] = dot(query[:, at], out_grad[:, at], 0, 0)

    send_states(1, make_qg)

    def finish_forward(unit, carry):
        inv = jnp.concatenate([acc_sq[...]] * 2, axis=1)
        lo[:, cols(unit)] = (att[:, cols(unit)] * inv * gain_ref[:, cols(unit)]).astype(BF16)
        return carry

    lax.fori_loop(0, units, finish_forward, 0)
    write_lo = pltpu.make_async_copy(lo, lo_hbm, out_sem.at[0])
    write_lo.start()

    def own_grads(unit, carry):
        query, key, value = q[:, cols(unit)], k[:, cols(unit)], v[:, cols(unit)]
        grad = og[:, cols(unit)]
        from_prefix = dot(grad, prefix[unit], 1, 1)
        for n in range(2):
            at = slice(n * HD, (n + 1) * HD)
            qh, kh, vh, gh = query[:, at], key[:, at], value[:, at], grad[:, at]
            g00 = masked(dot(gh[:tile], vh[:tile], 1, 1))
            g10 = dot(gh[tile:], vh[:tile], 1, 1).astype(BF16)
            g11 = masked(dot(gh[tile:], vh[tile:], 1, 1))
            w00 = weights[2 * unit + n, 0]
            w10 = weights[2 * unit + n, 1]
            w11 = weights[2 * unit + n, 2]
            where = pl.ds(pl.multiple_of(unit * PAIR + n * HD, HD), HD)
            gq[:tile, where] = (from_prefix[:tile, at] + dot(g00, kh[:tile], 1, 0)).astype(BF16)
            gq[tile:, where] = (
                from_prefix[tile:, at] + dot(jnp.concatenate([g10, g11], axis=1), kh, 1, 0)
            ).astype(BF16)
            part_k[:tile, where] = dot(jnp.concatenate([g00, g10], axis=0), qh, 0, 0)
            part_k[tile:, where] = dot(g11, qh[tile:], 0, 0)
            part_v[:tile, where] = dot(jnp.concatenate([w00, w10], axis=0), gh, 0, 0)
            part_v[tile:, where] = dot(w11, gh[tile:], 0, 0)
        return carry

    lax.fori_loop(0, units, own_grads, 0)
    write_gq = pltpu.make_async_copy(gq, gq_hbm, out_sem.at[1])
    write_gq.start()

    def write_grad(which, unit):
        source, target = ((gk, gk_hbm), (gv, gv_hbm))[which]
        return pltpu.make_async_copy(
            source.at[:, cols(unit)], target.at[:, cols(unit)], grad_sem.at[which, unit]
        )

    def add_suffix(unit, low):
        at = cols(unit)
        gk[:, at] = (part_k[:, at] + dot(v[:, at], low, 1, 1)).astype(BF16)
        write_grad(0, unit).start()
        gv[:, at] = (part_v[:, at] + dot(k[:, at], low, 1, 0)).astype(BF16)
        write_grad(1, unit).start()

    take_states(1, add_suffix)

    def end_writes(unit, carry):
        write_grad(0, unit).wait()
        write_grad(1, unit).wait()
        return carry

    end_sends(0)
    end_sends(1)
    for d in range(1, head_size):
        stat_copy(d).wait_send()
    write_lo.wait()
    write_gq.wait()
    lax.fori_loop(0, units, end_writes, 0)


def per_device(seq_size, head_size, queries, key_vectors, value_vectors, norm_gain, cotangent):
    tokens, columns = queries.shape
    heads = columns // HD
    units = heads // 2
    half = units // 2
    chips = seq_size // 2
    dma = pltpu.SemaphoreType.DMA
    anywhere = pl.BlockSpec(memory_space=pl.ANY)
    narrow = pltpu.VMEM((tokens, columns), BF16)
    wide = pltpu.VMEM((tokens, columns), F32)
    out = jax.ShapeDtypeStruct((tokens, columns), BF16)
    return pl.pallas_call(
        functools.partial(kernel, seq_size, head_size),
        out_shape=(out,) * 4,
        in_specs=[anywhere] * 3 + [pl.BlockSpec(memory_space=pltpu.VMEM), anywhere],
        out_specs=(anywhere,) * 4,
        scratch_shapes=[narrow] * 8
        + [
            pltpu.VMEM((heads, 3, tokens // 2, tokens // 2), BF16),
            wide,
            narrow,
            wide,
            wide,
            pltpu.VMEM((2, heads, HD, HD), F32),
            pltpu.VMEM((2, heads, HD, HD), F32),
            pltpu.VMEM((2, heads // 2, HD, HD), F32),
            pltpu.VMEM((2, max(chips - 1, 1), heads // 2, HD, HD), F32),
            pltpu.VMEM((2, heads, HD, HD), F32),
            pltpu.VMEM((units, PAIR, PAIR), BF16),
            pltpu.VMEM((tokens, HD), F32),
            pltpu.VMEM((tokens, HD), F32),
            pltpu.VMEM((8, tokens), F32),
            pltpu.VMEM((max(head_size - 1, 1), 8, tokens), F32),
            dma((2, units)),
            dma((2,)),
            dma((2,)),
            dma((2, units)),
            dma((2, units)),
            dma((2, units)),
            dma((2, max(chips - 1, 1), half)),
            dma((2, max(chips - 1, 1), half)),
            dma((2, half)),
            dma((2, half)),
            dma((max(head_size - 1, 1),)),
            dma((max(head_size - 1, 1),)),
        ],
        compiler_params=pltpu.CompilerParams(
            collective_id=0, has_side_effects=True, vmem_limit_bytes=60 * 1024 * 1024
        ),
        cost_estimate=pl.CostEstimate(
            flops=12 * tokens * tokens * columns,
            bytes_accessed=16 * tokens * columns,
            transcendentals=tokens,
        ),
    )(queries, key_vectors, value_vectors, norm_gain.reshape(1, columns), cotangent)


def solution(mesh):
    rows, features = P(("dp", "seq"), "head"), P("head")
    return jax.shard_map(
        functools.partial(per_device, mesh.shape["seq"], mesh.shape["head"]),
        mesh=mesh,
        in_specs=(rows, rows, rows, features, rows),
        out_specs=(rows,) * 4,
        check_vma=False,
    )
```

time: 219 us -> 51 us (0.23)
  waiting for transfers between devices: 81 us -> 0 us
  matrix products: 55.4 us -> 0 us
  Pallas kernels: 0 us -> 40.8 us
  local copies, waits for them, and re-layouts: 46.4 us -> 9.32 us
  starting transfers between devices: 18.8 us -> 0 us
  other arithmetic: 11.3 us -> 0 us
  blocking collectives: 3.97 us -> 0 us
    ppermute x6 -> x0, waiting for transfers between devices: 81 us -> none  [from_behind(): return lax.ppermute(block, axis, route)]
    dot_general x12 -> x0, matrix products: 55.4 us -> none  [the longest x1 8.24 us: per_device(): jnp.einsum('nhts,nshe->nthe', block_weights, value_blocks, preferred_elem...]
    pallas_call x0 -> x1, Pallas kernels: none -> 40.8 us  [per_device(): pl.pallas_call(functools.partial(kernel, seq_size, head_size), out_shape=...]
    ppermute x6 -> x0, starting transfers between devices: 18.8 us -> none  [from_behind(): return lax.ppermute(block, axis, route)]
    while x30 -> x0, local copies, waits for them, and re-layouts: 11.7 us -> none
    reshape x2 -> x0, local copies, waits for them, and re-layouts: 9.67 us -> none  [the longest x1 5.41 us: per_device(): attended = attended.reshape(tokens_here, features)]
    another operation x2 -> x0, local copies, waits for them, and re-layouts: 7.98 us -> none
    unnamed x27 -> x10, local copies, waits for them, and re-layouts: 17.1 us -> 9.32 us
  transfers between devices with their start and end apart: 6 -> 0, of which waited for: 6 -> 0; matrix products, arithmetic and copies ran while one was open for 0% -> 0% of each run, Pallas kernels for 0% -> 0%
where the time goes in v1:
time: 51 us; the launch traced here: 50.8 us
  Pallas kernels  40.8 us (80%)
  local copies, waits for them, and re-layouts  9.32 us (18%)
  between operations  0.65 us (1%)
    pallas_call x1, Pallas kernels, per_device(): pl.pallas_call(functools.partial(kernel, seq_size, head_size), out_shape=...  40.8 us
    unnamed x10, local copies, waits for them, and re-layouts  9.32 us

profile of v1, /device:TPU:1, one launch (start us, length us, event | category | flops | bytes accessed | tf_op | source)
XLA Modules:
  0.0 50.8 jit_solution(10372052433558835449)
XLA Ops:
  0.6 40.8 %shard_map.84 = (bf16[512,2048]{1,0:T(8,128)(2,1)}, bf16[512,2048]{1,0:T(8,128)(2,1)}, bf16[512,2048]{1,0:T(8,128)(2,1)}, bf16[512,2048]{1,0:T(8,128)(2,1)}) custom-call(bf16[512,2048]{1,0:T(8,128)(2,1)} %q_hbm.1, bf16[512,2048]{1,0:T(8,128)(2,1)} %k_hbm.1, bf16[512,2048]{1,0:T(8,128)(2,1)} %v_hbm.1, f32[1,2048]{1,0:T(1,128)} %bitcast.1, ...), custom_call_target="tpu_custom_call" | custom-call | flops 6442450944 | bytes 16777216 | tf_op jit(solution)/shard_map/pallas_call | solution.py:396
  41.5 0.0 copy-start.2
  41.5 3.3 %copy.13 = bf16[512,2048]{1,0:T(8,128)(2,1)} copy(bf16[512,2048]{1,0:T(8,128)(2,1)} %get-tuple-element.8) | data formatting | bytes 4194304
  44.8 0.0 copy-done.2
  44.8 0.0 copy-start.1
  44.8 1.3 %copy.14 = bf16[512,2048]{1,0:T(8,128)(2,1)} copy(bf16[512,2048]{1,0:T(8,128)(2,1)S(1)} %copy-done.2) | data formatting | bytes 4194304
  46.1 1.0 %copy-done.1 = bf16[512,2048]{1,0:T(8,128)(2,1)S(1)} copy-done((bf16[512,2048]{1,0:T(8,128)(2,1)S(1)}, bf16[512,2048]{1,0:T(8,128)(2,1)}, u32[]{:S(2)}) %copy-start.1) | copy-done | bytes 2097176
  47.1 0.0 copy-start
  47.1 1.3 %copy.15 = bf16[512,2048]{1,0:T(8,128)(2,1)} copy(bf16[512,2048]{1,0:T(8,128)(2,1)S(1)} %copy-done.1) | data formatting | bytes 4194304
  48.4 1.0 %copy-done = bf16[512,2048]{1,0:T(8,128)(2,1)S(1)} copy-done((bf16[512,2048]{1,0:T(8,128)(2,1)S(1)}, bf16[512,2048]{1,0:T(8,128)(2,1)}, u32[]{:S(2)}) %copy-start) | copy-done | bytes 2097176
  49.5 1.3 %copy.16 = bf16[512,2048]{1,0:T(8,128)(2,1)} copy(bf16[512,2048]{1,0:T(8,128)(2,1)S(1)} %copy-done) | data formatting | bytes 4194304
Async XLA Ops:
  41.5 3.3 %copy-start.2 = (bf16[512,2048]{1,0:T(8,128)(2,1)S(1)}, bf16[512,2048]{1,0:T(8,128)(2,1)}, u32[]{:S(2)}) copy-start(bf16[512,2048]{1,0:T(8,128)(2,1)} %get-tuple-element.9) | copy-start | bytes 6291460
  44.8 2.3 %copy-start.1 = (bf16[512,2048]{1,0:T(8,128)(2,1)S(1)}, bf16[512,2048]{1,0:T(8,128)(2,1)}, u32[]{:S(2)}) copy-start(bf16[512,2048]{1,0:T(8,128)(2,1)} %get-tuple-element.10) | copy-start | bytes 6291460
  47.1 2.3 %copy-start = (bf16[512,2048]{1,0:T(8,128)(2,1)S(1)}, bf16[512,2048]{1,0:T(8,128)(2,1)}, u32[]{:S(2)}) copy-start(bf16[512,2048]{1,0:T(8,128)(2,1)} %get-tuple-element.11) | copy-start | bytes 6291460

commit v2 on v1

--- a/solution.py
+++ b/solution.py
@@ -30,11 +30,11 @@
 def kernel(
     seq_size, head_size,
     q_hbm, k_hbm, v_hbm, gain_ref, ct_hbm,
-    lo_hbm, gq_hbm, gk_hbm, gv_hbm,
-    q, k, v, ct, lo, gq, gk, gv,
-    weights, att, og, part_k, part_v,
+    lo, gq, gk, gv,
+    q, k, v, ct,
+    weights, att, og, part_v,
     local, inner_in, total, cross_in, outer, prefix, acc_sq, acc_in, stat_out, stat_in,
-    kv_sem, in_sem, out_sem, grad_sem,
+    kv_sem, in_sem,
     in_send, in_recv, cross_send, cross_recv, fwd_send, fwd_recv, stat_send, stat_recv,
 ):
     tokens, columns = q.shape
@@ -64,15 +64,14 @@
         )
 
     def start_load(i, carry):
-        load(i, 0).start()
-        load(i, 1).start()
+        for n in (i, half + i):
+            load(n, 0).start()
+            load(n, 1).start()
         return carry
 
-    lax.fori_loop(0, units, start_load, 0)
+    lax.fori_loop(0, half, start_load, 0)
     load_q = pltpu.make_async_copy(q_hbm, q, in_sem.at[0])
     load_ct = pltpu.make_async_copy(ct_hbm, ct, in_sem.at[1])
-    load_q.start()
-    load_ct.start()
 
     barrier = pltpu.get_barrier_semaphore()
     pl.semaphore_signal(barrier, inc=1, device_id={"seq": partner}, device_id_type=MESH)
@@ -134,20 +133,23 @@
         return core == 0 if way == 0 else core == 1
 
     def send_states(way, make):
-        def partner_half(i, carry):
+        def give_other(i):
             make(i, other_unit(i))
             to_partner(way, i).start()
-            return carry
-
-        lax.fori_loop(0, half, partner_half, 0)
-
-        def own_half(j, carry):
+
+        give_other(0)
+
+        def step(j, carry):
             unit = own_unit(j)
             make(half + j, unit)
 
             @pl.when(gives_inner(way))
             def _():
                 to_partner(way, half + j).start()
+
+            @pl.when(j + 1 < half)
+            def _():
+                give_other(j + 1)
 
             to_partner(way, j).wait_recv()
             total[way, states(j)] = local[way, states(unit)] + inner_in[way, states(unit)]
@@ -159,7 +161,7 @@
 
             return carry
 
-        lax.fori_loop(0, half, own_half, 0)
+        lax.fori_loop(0, half, step, 0)
 
     def take_states(way, use):
         def step(j, carry):
@@ -234,6 +236,8 @@
             local[0, 2 * unit + n] = dot(key[:, at], value[:, at], 0, 0)
 
     send_states(0, make_kv)
+    load_q.start()
+    load_ct.start()
 
     causal = lax.broadcasted_iota(jnp.int32, (tile, tile), 0) >= lax.broadcasted_iota(
         jnp.int32, (tile, tile), 1
@@ -322,8 +326,7 @@
         return carry
 
     lax.fori_loop(0, units, finish_forward, 0)
-    write_lo = pltpu.make_async_copy(lo, lo_hbm, out_sem.at[0])
-    write_lo.start()
+    part_k = att
 
     def own_grads(unit, carry):
         query, key, value = q[:, cols(unit)], k[:, cols(unit)], v[:, cols(unit)]
@@ -350,36 +353,18 @@
         return carry
 
     lax.fori_loop(0, units, own_grads, 0)
-    write_gq = pltpu.make_async_copy(gq, gq_hbm, out_sem.at[1])
-    write_gq.start()
-
-    def write_grad(which, unit):
-        source, target = ((gk, gk_hbm), (gv, gv_hbm))[which]
-        return pltpu.make_async_copy(
-            source.at[:, cols(unit)], target.at[:, cols(unit)], grad_sem.at[which, unit]
-        )
 
     def add_suffix(unit, low):
         at = cols(unit)
         gk[:, at] = (part_k[:, at] + dot(v[:, at], low, 1, 1)).astype(BF16)
-        write_grad(0, unit).start()
         gv[:, at] = (part_v[:, at] + dot(k[:, at], low, 1, 0)).astype(BF16)
-        write_grad(1, unit).start()
 
     take_states(1, add_suffix)
-
-    def end_writes(unit, carry):
-        write_grad(0, unit).wait()
-        write_grad(1, unit).wait()
-        return carry
 
     end_sends(0)
     end_sends(1)
     for d in range(1, head_size):
         stat_copy(d).wait_send()
-    write_lo.wait()
-    write_gq.wait()
-    lax.fori_loop(0, units, end_writes, 0)
 
 
 def per_device(seq_size, head_size, queries, key_vectors, value_vectors, norm_gain, cotangent):
@@ -389,21 +374,19 @@
     half = units // 2
     chips = seq_size // 2
     dma = pltpu.SemaphoreType.DMA
-    anywhere = pl.BlockSpec(memory_space=pl.ANY)
+    in_hbm = pl.BlockSpec(memory_space=pltpu.HBM)
     narrow = pltpu.VMEM((tokens, columns), BF16)
     wide = pltpu.VMEM((tokens, columns), F32)
-    out = jax.ShapeDtypeStruct((tokens, columns), BF16)
     return pl.pallas_call(
         functools.partial(kernel, seq_size, head_size),
-        out_shape=(out,) * 4,
-        in_specs=[anywhere] * 3 + [pl.BlockSpec(memory_space=pltpu.VMEM), anywhere],
-        out_specs=(anywhere,) * 4,
-        scratch_shapes=[narrow] * 8
+        out_shape=(narrow,) * 4,
+        in_specs=[in_hbm] * 3 + [pl.BlockSpec(memory_space=pltpu.VMEM), in_hbm],
+        out_specs=(pl.BlockSpec(memory_space=pltpu.VMEM),) * 4,
+        scratch_shapes=[narrow] * 4
         + [
             pltpu.VMEM((heads, 3, tokens // 2, tokens // 2), BF16),
             wide,
             narrow,
-            wide,
             wide,
             pltpu.VMEM((2, heads, HD, HD), F32),
             pltpu.VMEM((2, heads, HD, HD), F32),
@@ -417,8 +400,6 @@
             pltpu.VMEM((max(head_size - 1, 1), 8, tokens), F32),
             dma((2, units)),
             dma((2,)),
-            dma((2,)),
-            dma((2, units)),
             dma((2, units)),
             dma((2, units)),
             dma((2, max(chips - 1, 1), half)),
@@ -429,7 +410,7 @@
             dma((max(head_size - 1, 1),)),
         ],
         compiler_params=pltpu.CompilerParams(
-            collective_id=0, has_side_effects=True, vmem_limit_bytes=60 * 1024 * 1024
+            collective_id=0, has_side_effects=True, vmem_limit_bytes=48 * 1024 * 1024
         ),
         cost_estimate=pl.CostEstimate(
             flops=12 * tokens * tokens * columns,

time: 51 us -> 46.8 us (0.918)
  local copies, waits for them, and re-layouts: 9.32 us -> 5.28 us
    unnamed x10 -> x4, local copies, waits for them, and re-layouts: 9.32 us -> 5.28 us
where the time goes in v2:
time: 46.8 us; the launch traced here: 46.3 us
  Pallas kernels  40.4 us (86%)
  local copies, waits for them, and re-layouts  5.28 us (11%)
  between operations  0.64 us (1%)
    pallas_call x1, Pallas kernels, per_device(): pl.pallas_call(functools.partial(kernel, seq_size, head_size), out_shape=...  40.4 us
    unnamed x4, local copies, waits for them, and re-layouts  5.28 us

profile of v2, /device:TPU:1, one launch (start us, length us, event | category | flops | bytes accessed | tf_op | source)
XLA Modules:
  0.0 46.3 jit_solution(6184457636608902013)
XLA Ops:
  0.6 40.4 %shard_map.84 = (bf16[512,2048]{1,0:T(8,128)(2,1)S(1)}, bf16[512,2048]{1,0:T(8,128)(2,1)S(1)}, bf16[512,2048]{1,0:T(8,128)(2,1)S(1)}, bf16[512,2048]{1,0:T(8,128)(2,1)S(1)}) custom-call(bf16[512,2048]{1,0:T(8,128)(2,1)} %q_hbm.1, bf16[512,2048]{1,0:T(8,128)(2,1)} %k_hbm.1, bf16[512,2048]{1,0:T(8,128)(2,1)} %v_hbm.1, f32[1,2048]{1,0:T(1,128)} %bitcast.1, ...), custom_call_target="tpu_custom_call" | custom-call | flops 6442450944 | bytes 16777216 | tf_op jit(solution)/shard_map/pallas_call | solution.py:380
  41.0 1.3 %copy.13 = bf16[512,2048]{1,0:T(8,128)(2,1)} copy(bf16[512,2048]{1,0:T(8,128)(2,1)S(1)} %get-tuple-element.4) | data formatting | bytes 4194304
  42.3 1.3 %copy.14 = bf16[512,2048]{1,0:T(8,128)(2,1)} copy(bf16[512,2048]{1,0:T(8,128)(2,1)S(1)} %get-tuple-element.5) | data formatting | bytes 4194304
  43.7 1.3 %copy.15 = bf16[512,2048]{1,0:T(8,128)(2,1)} copy(bf16[512,2048]{1,0:T(8,128)(2,1)S(1)} %get-tuple-element.6) | data formatting | bytes 4194304
  45.0 1.3 %copy.16 = bf16[512,2048]{1,0:T(8,128)(2,1)} copy(bf16[512,2048]{1,0:T(8,128)(2,1)S(1)} %get-tuple-element.7) | data formatting | bytes 4194304

commit v3 on v2

--- a/solution.py
+++ b/solution.py
@@ -32,7 +32,7 @@
     q_hbm, k_hbm, v_hbm, gain_ref, ct_hbm,
     lo, gq, gk, gv,
     q, k, v, ct,
-    weights, att, og, part_v,
+    weights, q_turned, att, og, part_v,
     local, inner_in, total, cross_in, outer, prefix, acc_sq, acc_in, stat_out, stat_in,
     kv_sem, in_sem,
     in_send, in_recv, cross_send, cross_recv, fwd_send, fwd_recv, stat_send, stat_recv,
@@ -239,12 +239,8 @@
     load_q.start()
     load_ct.start()
 
-    causal = lax.broadcasted_iota(jnp.int32, (tile, tile), 0) >= lax.broadcasted_iota(
-        jnp.int32, (tile, tile), 1
-    )
-
-    def masked(scores):
-        return jnp.where(causal, scores, 0.0).astype(BF16)
+    row = lax.broadcasted_iota(jnp.int32, (tile, tile), 0)
+    column = lax.broadcasted_iota(jnp.int32, (tile, tile), 1)
 
     acc_sq[...] = jnp.zeros_like(acc_sq)
     acc_in[...] = jnp.zeros_like(acc_in)
@@ -255,15 +251,16 @@
         for n in range(2):
             at = slice(n * HD, (n + 1) * HD)
             qh, kh, vh = query[:, at], key[:, at], value[:, at]
-            w00 = masked(dot(qh[:tile], kh[:tile], 1, 1))
-            w10 = dot(qh[tile:], kh[:tile], 1, 1).astype(BF16)
-            w11 = masked(dot(qh[tile:], kh[tile:], 1, 1))
+            w00 = jnp.where(row <= column, dot(kh[:tile], qh[:tile], 1, 1), 0.0).astype(BF16)
+            w01 = dot(kh[:tile], qh[tile:], 1, 1).astype(BF16)
+            w11 = jnp.where(row <= column, dot(kh[tile:], qh[tile:], 1, 1), 0.0).astype(BF16)
             weights[2 * unit + n, 0] = w00
-            weights[2 * unit + n, 1] = w10
+            weights[2 * unit + n, 1] = w01
             weights[2 * unit + n, 2] = w11
             where = pl.ds(pl.multiple_of(unit * PAIR + n * HD, HD), HD)
-            att[:tile, where] = dot(w00, vh[:tile], 1, 0)
-            att[tile:, where] = dot(jnp.concatenate([w10, w11], axis=1), vh, 1, 0)
+            att[:tile, where] = dot(w00, vh[:tile], 0, 0)
+            att[tile:, where] = dot(jnp.concatenate([w01, w11], axis=0), vh, 0, 0)
+        q_turned[unit] = query.T
         return carry
 
     lax.fori_loop(0, units, own_scores, 0)
@@ -313,33 +310,29 @@
         scaled = ct[:, cols(unit)].astype(F32) * gain
         out_grad = (inv * scaled - attended * coef).astype(BF16)
         og[:, cols(unit)] = out_grad
-        query = q[:, cols(unit)]
+        turned = q_turned[unit]
         for n in range(2):
             at = slice(n * HD, (n + 1) * HD)
-            local[1, 2 * unit + n] = dot(query[:, at], out_grad[:, at], 0, 0)
+            local[1, 2 * unit + n] = dot(turned[at], out_grad[:, at], 1, 0)
 
     send_states(1, make_qg)
 
-    def finish_forward(unit, carry):
-        inv = jnp.concatenate([acc_sq[...]] * 2, axis=1)
-        lo[:, cols(unit)] = (att[:, cols(unit)] * inv * gain_ref[:, cols(unit)]).astype(BF16)
-        return carry
-
-    lax.fori_loop(0, units, finish_forward, 0)
     part_k = att
 
     def own_grads(unit, carry):
         query, key, value = q[:, cols(unit)], k[:, cols(unit)], v[:, cols(unit)]
         grad = og[:, cols(unit)]
+        inv = jnp.concatenate([acc_sq[...]] * 2, axis=1)
+        lo[:, cols(unit)] = (att[:, cols(unit)] * inv * gain_ref[:, cols(unit)]).astype(BF16)
         from_prefix = dot(grad, prefix[unit], 1, 1)
         for n in range(2):
             at = slice(n * HD, (n + 1) * HD)
             qh, kh, vh, gh = query[:, at], key[:, at], value[:, at], grad[:, at]
-            g00 = masked(dot(gh[:tile], vh[:tile], 1, 1))
+            g00 = jnp.where(row >= column, dot(gh[:tile], vh[:tile], 1, 1), 0.0).astype(BF16)
             g10 = dot(gh[tile:], vh[:tile], 1, 1).astype(BF16)
-            g11 = masked(dot(gh[tile:], vh[tile:], 1, 1))
+            g11 = jnp.where(row >= column, dot(gh[tile:], vh[tile:], 1, 1), 0.0).astype(BF16)
             w00 = weights[2 * unit + n, 0]
-            w10 = weights[2 * unit + n, 1]
+            w01 = weights[2 * unit + n, 1]
             w11 = weights[2 * unit + n, 2]
             where = pl.ds(pl.multiple_of(unit * PAIR + n * HD, HD), HD)
             gq[:tile, where] = (from_prefix[:tile, at] + dot(g00, kh[:tile], 1, 0)).astype(BF16)
@@ -348,8 +341,8 @@
             ).astype(BF16)
             part_k[:tile, where] = dot(jnp.concatenate([g00, g10], axis=0), qh, 0, 0)
             part_k[tile:, where] = dot(g11, qh[tile:], 0, 0)
-            part_v[:tile, where] = dot(jnp.concatenate([w00, w10], axis=0), gh, 0, 0)
-            part_v[tile:, where] = dot(w11, gh[tile:], 0, 0)
+            part_v[:tile, where] = dot(jnp.concatenate([w00, w01], axis=1), gh, 1, 0)
+            part_v[tile:, where] = dot(w11, gh[tile:], 1, 0)
         return carry
 
     lax.fori_loop(0, units, own_grads, 0)
@@ -365,6 +358,22 @@
     end_sends(1)
     for d in range(1, head_size):
         stat_copy(d).wait_send()
+
+
+def write_out(*refs):
+    sources, targets, sems = refs[:4], refs[4:8], refs[8]
+    rows = sources[0].shape[0] // 4
+    copies = [
+        pltpu.make_async_copy(
+            source.at[pl.ds(part * rows, rows)], target.at[pl.ds(part * rows, rows)], sems.at[n, part]
+        )
+        for part in range(4)
+        for n, (source, target) in enumerate(zip(sources, targets))
+    ]
+    for copy in copies:
+        copy.start()
+    for copy in copies:
+        copy.wait()
 
 
 def per_device(seq_size, head_size, queries, key_vectors, value_vectors, norm_gain, cotangent):
@@ -377,7 +386,7 @@
     in_hbm = pl.BlockSpec(memory_space=pltpu.HBM)
     narrow = pltpu.VMEM((tokens, columns), BF16)
     wide = pltpu.VMEM((tokens, columns), F32)
-    return pl.pallas_call(
+    results = pl.pallas_call(
         functools.partial(kernel, seq_size, head_size),
         out_shape=(narrow,) * 4,
         in_specs=[in_hbm] * 3 + [pl.BlockSpec(memory_space=pltpu.VMEM), in_hbm],
@@ -385,6 +394,7 @@
         scratch_shapes=[narrow] * 4
         + [
             pltpu.VMEM((heads, 3, tokens // 2, tokens // 2), BF16),
+            pltpu.VMEM((units, PAIR, tokens), BF16),
             wide,
             narrow,
             wide,
@@ -418,6 +428,17 @@
             transcendentals=tokens,
         ),
     )(queries, key_vectors, value_vectors, norm_gain.reshape(1, columns), cotangent)
+    out = jax.ShapeDtypeStruct((tokens, columns), BF16)
+    return pl.pallas_call(
+        write_out,
+        out_shape=(out,) * 4,
+        in_specs=[pl.BlockSpec(memory_space=pltpu.VMEM)] * 4,
+        out_specs=(pl.BlockSpec(memory_space=pltpu.HBM),) * 4,
+        scratch_shapes=[dma((4, 4))],
+        cost_estimate=pl.CostEstimate(
+            flops=0, bytes_accessed=8 * tokens * columns, transcendentals=0
+        ),
+    )(*results)
 
 
 def solution(mesh):

time: 46.8 us -> 55 us (1.18)
  Pallas kernels: 40.4 us -> 48.8 us
    pallas_call x0 -> x1, Pallas kernels: none -> 6.88 us  [per_device(): pl.pallas_call(write_out, out_shape=(out,) * 4, in_specs=[pl.BlockSpec(me...]
    pallas_call x1, Pallas kernels: 40.4 us -> 41.9 us  [per_device(): pl.pallas_call(functools.partial(kernel, seq_size, head_size), out_shape=...]
    unnamed x4 -> x8, local copies, waits for them, and re-layouts: 5.28 us -> 5.29 us
where the time goes in v3:
time: 55 us; the launch traced here: 54.7 us
  Pallas kernels  48.8 us (89%)
  local copies, waits for them, and re-layouts  5.29 us (10%)
  between operations  0.65 us (1%)
    pallas_call x1, Pallas kernels, per_device(): pl.pallas_call(functools.partial(kernel, seq_size, head_size), out_shape=...  41.9 us
    pallas_call x1, Pallas kernels, per_device(): pl.pallas_call(write_out, out_shape=(out,) * 4, in_specs=[pl.BlockSpec(me...  6.88 us
    unnamed x8, local copies, waits for them, and re-layouts  5.29 us

profile of v3, /device:TPU:1, one launch (start us, length us, event | category | flops | bytes accessed | tf_op | source)
XLA Modules:
  0.0 54.7 jit_solution(15317198246089549570)
XLA Ops:
  0.6 41.9 %shard_map.84 = (bf16[512,2048]{1,0:T(8,128)(2,1)S(1)}, bf16[512,2048]{1,0:T(8,128)(2,1)S(1)}, bf16[512,2048]{1,0:T(8,128)(2,1)S(1)}, bf16[512,2048]{1,0:T(8,128)(2,1)S(1)}) custom-call(bf16[512,2048]{1,0:T(8,128)(2,1)} %q_hbm.1, bf16[512,2048]{1,0:T(8,128)(2,1)} %k_hbm.1, bf16[512,2048]{1,0:T(8,128)(2,1)} %v_hbm.1, f32[1,2048]{1,0:T(1,128)} %bitcast.1, ...), custom_call_target="tpu_custom_call" | custom-call | flops 6442450944 | bytes 16777216 | tf_op jit(solution)/shard_map/pallas_call | solution.py:389
  42.5 0.0 copy-start
  42.5 1.3 %copy-done = bf16[512,2048]{1,0:T(8,128)(2,1)} copy-done((bf16[512,2048]{1,0:T(8,128)(2,1)}, bf16[512,2048]{1,0:T(8,128)(2,1)S(1)}, u32[]{:S(2)}) %copy-start) | copy-done | bytes 2097176
  43.9 0.0 copy-start.1
  43.9 1.3 %copy-done.1 = bf16[512,2048]{1,0:T(8,128)(2,1)} copy-done((bf16[512,2048]{1,0:T(8,128)(2,1)}, bf16[512,2048]{1,0:T(8,128)(2,1)S(1)}, u32[]{:S(2)}) %copy-start.1) | copy-done | bytes 2097176
  45.2 0.0 copy-start.2
  45.2 1.3 %copy-done.2 = bf16[512,2048]{1,0:T(8,128)(2,1)} copy-done((bf16[512,2048]{1,0:T(8,128)(2,1)}, bf16[512,2048]{1,0:T(8,128)(2,1)S(1)}, u32[]{:S(2)}) %copy-start.2) | copy-done | bytes 2097176
  46.5 0.0 copy-start.3
  46.5 1.3 %copy-done.3 = bf16[512,2048]{1,0:T(8,128)(2,1)} copy-done((bf16[512,2048]{1,0:T(8,128)(2,1)}, bf16[512,2048]{1,0:T(8,128)(2,1)S(1)}, u32[]{:S(2)}) %copy-start.3) | copy-done | bytes 2097176
  47.8 6.9 %shard_map.85 = (bf16[512,2048]{1,0:T(8,128)(2,1)}, bf16[512,2048]{1,0:T(8,128)(2,1)}, bf16[512,2048]{1,0:T(8,128)(2,1)}, bf16[512,2048]{1,0:T(8,128)(2,1)}) custom-call(bf16[512,2048]{1,0:T(8,128)(2,1)} %copy-done, bf16[512,2048]{1,0:T(8,128)(2,1)} %copy-done.1, bf16[512,2048]{1,0:T(8,128)(2,1)} %copy-done.2, bf16[512,2048]{1,0:T(8,128)(2,1)} %copy-done.3), custom_call_target="tpu_custom_call" | custom-call | bytes 8388608 | tf_op jit(solution)/shard_map/pallas_call | solution.py:432
Async XLA Ops:
  42.5 1.3 %copy-start = (bf16[512,2048]{1,0:T(8,128)(2,1)}, bf16[512,2048]{1,0:T(8,128)(2,1)S(1)}, u32[]{:S(2)}) copy-start(bf16[512,2048]{1,0:T(8,128)(2,1)S(1)} %get-tuple-element.8.refs_0_) | copy-start | bytes 6291460
  43.9 1.3 %copy-start.1 = (bf16[512,2048]{1,0:T(8,128)(2,1)}, bf16[512,2048]{1,0:T(8,128)(2,1)S(1)}, u32[]{:S(2)}) copy-start(bf16[512,2048]{1,0:T(8,128)(2,1)S(1)} %get-tuple-element.9.refs_1_) | copy-start | bytes 6291460
  45.2 1.3 %copy-start.2 = (bf16[512,2048]{1,0:T(8,128)(2,1)}, bf16[512,2048]{1,0:T(8,128)(2,1)S(1)}, u32[]{:S(2)}) copy-start(bf16[512,2048]{1,0:T(8,128)(2,1)S(1)} %get-tuple-element.10.refs_2_) | copy-start | bytes 6291460
  46.5 1.3 %copy-start.3 = (bf16[512,2048]{1,0:T(8,128)(2,1)}, bf16[512,2048]{1,0:T(8,128)(2,1)S(1)}, u32[]{:S(2)}) copy-start(bf16[512,2048]{1,0:T(8,128)(2,1)S(1)} %get-tuple-element.11.refs_3_) | copy-start | bytes 6291460

commit v4 on v3

--- a/solution.py
+++ b/solution.py
@@ -32,7 +32,7 @@
     q_hbm, k_hbm, v_hbm, gain_ref, ct_hbm,
     lo, gq, gk, gv,
     q, k, v, ct,
-    weights, q_turned, att, og, part_v,
+    weights, att, og, part_v,
     local, inner_in, total, cross_in, outer, prefix, acc_sq, acc_in, stat_out, stat_in,
     kv_sem, in_sem,
     in_send, in_recv, cross_send, cross_recv, fwd_send, fwd_recv, stat_send, stat_recv,
@@ -72,6 +72,8 @@
     lax.fori_loop(0, half, start_load, 0)
     load_q = pltpu.make_async_copy(q_hbm, q, in_sem.at[0])
     load_ct = pltpu.make_async_copy(ct_hbm, ct, in_sem.at[1])
+    load_q.start()
+    load_ct.start()
 
     barrier = pltpu.get_barrier_semaphore()
     pl.semaphore_signal(barrier, inc=1, device_id={"seq": partner}, device_id_type=MESH)
@@ -227,20 +229,36 @@
 
         lax.fori_loop(0, half, step, 0)
 
+    def put_state(way, unit, both):
+        local[way, 2 * unit] = both[:HD, :HD]
+        local[way, 2 * unit + 1] = both[HD:, HD:]
+
     def make_kv(i, unit):
         load(i, 0).wait()
         load(i, 1).wait()
-        key, value = k[:, cols(unit)], v[:, cols(unit)]
-        for n in range(2):
-            at = slice(n * HD, (n + 1) * HD)
-            local[0, 2 * unit + n] = dot(key[:, at], value[:, at], 0, 0)
+        put_state(0, unit, dot(k[:, cols(unit)], v[:, cols(unit)], 0, 0))
 
     send_states(0, make_kv)
-    load_q.start()
-    load_ct.start()
-
-    row = lax.broadcasted_iota(jnp.int32, (tile, tile), 0)
-    column = lax.broadcasted_iota(jnp.int32, (tile, tile), 1)
+
+    def causal(scores):
+        row = lax.broadcasted_iota(jnp.int32, (tile, tile), 0)
+        column = lax.broadcasted_iota(jnp.int32, (tile, tile), 1)
+        return jnp.where(row >= column, scores, 0.0).astype(BF16)
+
+    def three_tiles(rows, columns):
+        left = dot(rows, columns[:tile], 1, 1)
+        right = dot(rows[tile:], columns[tile:], 1, 1)
+        return causal(left[:tile]), left[tile:].astype(BF16), causal(right)
+
+    def times(tiles, values):
+        t00, t10, t11 = tiles
+        first = dot(jnp.concatenate([t00, t10], axis=0), values[:tile], 1, 0)
+        return first[:tile], first[tile:] + dot(t11, values[tile:], 1, 0)
+
+    def turned_times(tiles, values):
+        t00, t10, t11 = tiles
+        second = dot(jnp.concatenate([t10, t11], axis=1), values[tile:], 0, 0)
+        return second[:tile] + dot(t00, values[:tile], 0, 0), second[tile:]
 
     acc_sq[...] = jnp.zeros_like(acc_sq)
     acc_in[...] = jnp.zeros_like(acc_in)
@@ -251,19 +269,14 @@
         for n in range(2):
             at = slice(n * HD, (n + 1) * HD)
             qh, kh, vh = query[:, at], key[:, at], value[:, at]
-            w00 = jnp.where(row <= column, dot(kh[:tile], qh[:tile], 1, 1), 0.0).astype(BF16)
-            w01 = dot(kh[:tile], qh[tile:], 1, 1).astype(BF16)
-            w11 = jnp.where(row <= column, dot(kh[tile:], qh[tile:], 1, 1), 0.0).astype(BF16)
-            weights[2 * unit + n, 0] = w00
-            weights[2 * unit + n, 1] = w01
-            weights[2 * unit + n, 2] = w11
+            tiles = three_tiles(qh, kh)
+            for m in range(3):
+                weights[2 * unit + n, m] = tiles[m]
             where = pl.ds(pl.multiple_of(unit * PAIR + n * HD, HD), HD)
-            att[:tile, where] = dot(w00, vh[:tile], 0, 0)
-            att[tile:, where] = dot(jnp.concatenate([w01, w11], axis=0), vh, 0, 0)
-        q_turned[unit] = query.T
+            att[:tile, where], att[tile:, where] = times(tiles, vh)
         return carry
 
-    lax.fori_loop(0, units, own_scores, 0)
+    lax.fori_loop(0, units, own_scores, 0, unroll=2)
     load_ct.wait()
 
     def add_prefix(unit, low):
@@ -310,10 +323,7 @@
         scaled = ct[:, cols(unit)].astype(F32) * gain
         out_grad = (inv * scaled - attended * coef).astype(BF16)
         og[:, cols(unit)] = out_grad
-        turned = q_turned[unit]
-        for n in range(2):
-            at = slice(n * HD, (n + 1) * HD)
-            local[1, 2 * unit + n] = dot(turned[at], out_grad[:, at], 1, 0)
+        put_state(1, unit, dot(q[:, cols(unit)], out_grad, 0, 0))
 
     send_states(1, make_qg)
 
@@ -328,24 +338,17 @@
         for n in range(2):
             at = slice(n * HD, (n + 1) * HD)
             qh, kh, vh, gh = query[:, at], key[:, at], value[:, at], grad[:, at]
-            g00 = jnp.where(row >= column, dot(gh[:tile], vh[:tile], 1, 1), 0.0).astype(BF16)
-            g10 = dot(gh[tile:], vh[:tile], 1, 1).astype(BF16)
-            g11 = jnp.where(row >= column, dot(gh[tile:], vh[tile:], 1, 1), 0.0).astype(BF16)
-            w00 = weights[2 * unit + n, 0]
-            w01 = weights[2 * unit + n, 1]
-            w11 = weights[2 * unit + n, 2]
+            tiles = three_tiles(gh, vh)
+            kept = [weights[2 * unit + n, m] for m in range(3)]
             where = pl.ds(pl.multiple_of(unit * PAIR + n * HD, HD), HD)
-            gq[:tile, where] = (from_prefix[:tile, at] + dot(g00, kh[:tile], 1, 0)).astype(BF16)
-            gq[tile:, where] = (
-                from_prefix[tile:, at] + dot(jnp.concatenate([g10, g11], axis=1), kh, 1, 0)
-            ).astype(BF16)
-            part_k[:tile, where] = dot(jnp.concatenate([g00, g10], axis=0), qh, 0, 0)
-            part_k[tile:, where] = dot(g11, qh[tile:], 0, 0)
-            part_v[:tile, where] = dot(jnp.concatenate([w00, w01], axis=1), gh, 1, 0)
-            part_v[tile:, where] = dot(w11, gh[tile:], 1, 0)
+            upper, lower = times(tiles, kh)
+            gq[:tile, where] = (from_prefix[:tile, at] + upper).astype(BF16)
+            gq[tile:, where] = (from_prefix[tile:, at] + lower).astype(BF16)
+            part_k[:tile, where], part_k[tile:, where] = turned_times(tiles, qh)
+            part_v[:tile, where], part_v[tile:, where] = turned_times(kept, gh)
         return carry
 
-    lax.fori_loop(0, units, own_grads, 0)
+    lax.fori_loop(0, units, own_grads, 0, unroll=2)
 
     def add_suffix(unit, low):
         at = cols(unit)
@@ -394,7 +397,6 @@
         scratch_shapes=[narrow] * 4
         + [
             pltpu.VMEM((heads, 3, tokens // 2, tokens // 2), BF16),
-            pltpu.VMEM((units, PAIR, tokens), BF16),
             wide,
             narrow,
             wide,
@@ -433,6 +435,7 @@
         write_out,
         out_shape=(out,) * 4,
         in_specs=[pl.BlockSpec(memory_space=pltpu.VMEM)] * 4,
+        compiler_params=pltpu.CompilerParams(vmem_limit_bytes=1024 * 1024),
         out_specs=(pl.BlockSpec(memory_space=pltpu.HBM),) * 4,
         scratch_shapes=[dma((4, 4))],
         cost_estimate=pl.CostEstimate(

time: 55 us -> 44.4 us (0.81)
  Pallas kernels: 48.8 us -> 43.5 us
  local copies, waits for them, and re-layouts: 5.29 us -> 0 us
    unnamed x8 -> x0, local copies, waits for them, and re-layouts: 5.29 us -> none
    pallas_call x1, Pallas kernels: 6.88 us -> 3.42 us  [per_device(): pl.pallas_call(write_out, out_shape=(out,) * 4, in_specs=[pl.BlockSpec(me...]
    pallas_call x1, Pallas kernels: 41.9 us -> 40.1 us  [per_device(): pl.pallas_call(functools.partial(kernel, seq_size, head_size), out_shape=...]
where the time goes in v4:
time: 44.4 us; the launch traced here: 44.1 us
  Pallas kernels  43.5 us (98%)
  between operations  0.64 us (1%)
    pallas_call x1, Pallas kernels, per_device(): pl.pallas_call(functools.partial(kernel, seq_size, head_size), out_shape=...  40.1 us
    pallas_call x1, Pallas kernels, per_device(): pl.pallas_call(write_out, out_shape=(out,) * 4, in_specs=[pl.BlockSpec(me...  3.42 us

profile of v4, /device:TPU:1, one launch (start us, length us, event | category | flops | bytes accessed | tf_op | source)
XLA Modules:
  0.0 44.1 jit_solution(8656780127023544891)
XLA Ops:
  0.6 40.1 %shard_map.84 = (bf16[512,2048]{1,0:T(8,128)(2,1)S(1)}, bf16[512,2048]{1,0:T(8,128)(2,1)S(1)}, bf16[512,2048]{1,0:T(8,128)(2,1)S(1)}, bf16[512,2048]{1,0:T(8,128)(2,1)S(1)}) custom-call(bf16[512,2048]{1,0:T(8,128)(2,1)} %q_hbm.1, bf16[512,2048]{1,0:T(8,128)(2,1)} %k_hbm.1, bf16[512,2048]{1,0:T(8,128)(2,1)} %v_hbm.1, f32[1,2048]{1,0:T(1,128)} %bitcast.1, ...), custom_call_target="tpu_custom_call" | custom-call | flops 6442450944 | bytes 16777216 | tf_op jit(solution)/shard_map/pallas_call | solution.py:392
  40.7 3.4 %shard_map.85 = (bf16[512,2048]{1,0:T(8,128)(2,1)}, bf16[512,2048]{1,0:T(8,128)(2,1)}, bf16[512,2048]{1,0:T(8,128)(2,1)}, bf16[512,2048]{1,0:T(8,128)(2,1)}) custom-call(bf16[512,2048]{1,0:T(8,128)(2,1)S(1)} %get-tuple-element.8.refs_0_, bf16[512,2048]{1,0:T(8,128)(2,1)S(1)} %get-tuple-element.9.refs_1_, bf16[512,2048]{1,0:T(8,128)(2,1)S(1)} %get-tuple-element.10.refs_2_, ...), custom_call_target="tpu_custom_call" | custom-call | bytes 8388608 | tf_op jit(solution)/shard_map/pallas_call | solution.py:434

commit v5 on v4

--- a/solution.py
+++ b/solution.py
@@ -69,11 +69,9 @@
             load(n, 1).start()
         return carry
 
-    lax.fori_loop(0, half, start_load, 0)
+    start_load(0, 0)
     load_q = pltpu.make_async_copy(q_hbm, q, in_sem.at[0])
     load_ct = pltpu.make_async_copy(ct_hbm, ct, in_sem.at[1])
-    load_q.start()
-    load_ct.start()
 
     barrier = pltpu.get_barrier_semaphore()
     pl.semaphore_signal(barrier, inc=1, device_id={"seq": partner}, device_id_type=MESH)
@@ -86,6 +84,9 @@
             barrier, inc=1, device_id={"head": lax.rem(head + d, head_size)}, device_id_type=MESH
         )
     pl.semaphore_wait(barrier, 1 + (chips - 1) + (head_size - 1))
+    lax.fori_loop(1, half, start_load, 0)
+    load_q.start()
+    load_ct.start()
 
     def states(unit):
         return pl.ds(2 * unit, 2)

time: 44.4 us -> 44.3 us (level)
  no operation moved by 1% of the time
where the time goes in v5:
time: 44.3 us; the launch traced here: 44.1 us
  Pallas kernels  43.5 us (98%)
  between operations  0.64 us (1%)
    pallas_call x1, Pallas kernels, per_device(): pl.pallas_call(functools.partial(kernel, seq_size, head_size), out_shape=...  40.1 us
    pallas_call x1, Pallas kernels, per_device(): pl.pallas_call(write_out, out_shape=(out,) * 4, in_specs=[pl.BlockSpec(me...  3.42 us

profile of v5, /device:TPU:1, one launch (start us, length us, event | category | flops | bytes accessed | tf_op | source)
XLA Modules:
  0.0 44.1 jit_solution(6999070468281270977)
XLA Ops:
  0.6 40.1 %shard_map.84 = (bf16[512,2048]{1,0:T(8,128)(2,1)S(1)}, bf16[512,2048]{1,0:T(8,128)(2,1)S(1)}, bf16[512,2048]{1,0:T(8,128)(2,1)S(1)}, bf16[512,2048]{1,0:T(8,128)(2,1)S(1)}) custom-call(bf16[512,2048]{1,0:T(8,128)(2,1)} %q_hbm.1, bf16[512,2048]{1,0:T(8,128)(2,1)} %k_hbm.1, bf16[512,2048]{1,0:T(8,128)(2,1)} %v_hbm.1, f32[1,2048]{1,0:T(1,128)} %bitcast.1, ...), custom_call_target="tpu_custom_call" | custom-call | flops 6442450944 | bytes 16777216 | tf_op jit(solution)/shard_map/pallas_call | solution.py:393
  40.7 3.4 %shard_map.85 = (bf16[512,2048]{1,0:T(8,128)(2,1)}, bf16[512,2048]{1,0:T(8,128)(2,1)}, bf16[512,2048]{1,0:T(8,128)(2,1)}, bf16[512,2048]{1,0:T(8,128)(2,1)}) custom-call(bf16[512,2048]{1,0:T(8,128)(2,1)S(1)} %get-tuple-element.8.refs_0_, bf16[512,2048]{1,0:T(8,128)(2,1)S(1)} %get-tuple-element.9.refs_1_, bf16[512,2048]{1,0:T(8,128)(2,1)S(1)} %get-tuple-element.10.refs_2_, ...), custom_call_target="tpu_custom_call" | custom-call | bytes 8388608 | tf_op jit(solution)/shard_map/pallas_call | solution.py:435
